TPU v7x, 768 devices: a whole 4x8x12 slice. The times are simulated.
768 devices in a mesh: dp: 24 (over z, core), node: 8 (over y), chip: 4 (over x).
Axes of the slice: x: 4, y: 8, z: 12, core: 2. Of those that a mesh axis runs over, the one named last changes fastest.
Arguments:
- tokens: bfloat16 [49152, 2048], P(('dp', 'node', 'chip')), parts along dimension 0, may hold values from -6 to 6
- expert_ids: int32 [49152, 8], P(('dp', 'node', 'chip')), parts along dimension 0, may hold values from 0 to 31, as said below
- gate_fixed: int32 [49152, 8], P(('dp', 'node', 'chip')), parts along dimension 0, may hold values from 1 to 255
- w_gate: bfloat16 [32, 2048, 768], P(('node', 'chip')), may hold values from -0.125 to 0.125
- w_up: bfloat16 [32, 2048, 768], P(('node', 'chip')), may hold values from -0.125 to 0.125
- w_down: bfloat16 [32, 768, 2048], P(('node', 'chip')), may hold values from -0.21875 to 0.21875
Outputs:
- mixed: bfloat16 [49152, 2048], P(('dp', 'node', 'chip')), parts along dimension 0
There are 24 independent parts, one for each index of `dp`. A program takes and returns all parts, laid end to end along the dimension named above; an argument that names none is the same for every part. Nothing has to cross between parts.
Inputs may be any that keep to these rules, and one draw needn't show every extreme that they name: `expert_ids`: each row names 8 different experts, all within at most 4 groups, expert e belonging to group e // 4. One expert is named by 16 or more tokens of every block of 64 tokens.
All inputs are finite; a program needn't handle non-finite values.
Results may differ from a plain program's by a relative error of at most 0.0057.
Values may be sent and summed in bfloat16 or wider, within the bound.
No kernel may reach another device: no remote copies, remote signals or barrier semaphores. Data moves between devices by JAX's collectives and lax.ppermute only.
A program may use at most 64 MiB of HBM per device.

v0:
```python
import jax
import jax.numpy as jnp
from jax import lax
from jax.sharding import PartitionSpec as P


def route_tables(ids_block, gates_block, experts, capacity):
    tok_dev, top_count = ids_block.shape
    routes = tok_dev * top_count
    slots = experts * capacity
    flat_ids = ids_block.reshape(routes)
    one_hot = (flat_ids[:, None] == jnp.arange(experts, dtype=jnp.int32)[None, :]).astype(jnp.int32)
    before = jnp.cumsum(one_hot, axis=0) - one_hot
    rank_in = jnp.sum(before * one_hot, axis=1)
    is_kept = rank_in < capacity
    slot_index = flat_ids * capacity + rank_in
    placed = (slot_index[:, None] == jnp.arange(slots, dtype=jnp.int32)[None, :]) & is_kept[:, None]
    dispatch_map = jnp.any(placed.reshape(tok_dev, top_count, slots), axis=1).T.astype(jnp.bfloat16)
    weights = gates_block.reshape(routes).astype(jnp.float32) / 256.0
    combine_map = jnp.sum(
        (placed.astype(jnp.float32) * weights[:, None]).reshape(tok_dev, top_count, slots), axis=1
    )
    return (dispatch_map, combine_map.astype(jnp.bfloat16))


def expert_ffn(arrived, gate_mat, up_mat, down_mat):
    width = arrived.shape[-1]
    row_block = arrived.reshape(-1, width)
    gate_act = jnp.dot(row_block, gate_mat, preferred_element_type=jnp.float32)
    up_act = jnp.dot(row_block, up_mat, preferred_element_type=jnp.float32)
    hidden = (jax.nn.silu(gate_act) * up_act).astype(jnp.bfloat16)
    output = jnp.dot(hidden, down_mat, preferred_element_type=jnp.float32).astype(jnp.bfloat16)
    return output.reshape(arrived.shape)


def on_device(tokens, expert_ids, gate_fixed, w_gate, w_up, w_down):
    tok_dev, width = tokens.shape
    top_count = expert_ids.shape[1]
    devices = lax.axis_size(("node", "chip"))
    experts = devices * w_gate.shape[0]
    capacity = tok_dev * top_count // experts
    dispatch_map, combine_map = route_tables(expert_ids, gate_fixed, experts, capacity)
    outbound = jnp.dot(dispatch_map, tokens, preferred_element_type=jnp.float32).astype(
        jnp.bfloat16
    )
    outbound = outbound.reshape(experts, capacity, width)
    served = expert_ffn(
        lax.all_to_all(outbound, ("node", "chip"), split_axis=0, concat_axis=0, tiled=True),
        w_gate[0],
        w_up[0],
        w_down[0],
    )
    results = lax.all_to_all(served, ("node", "chip"), split_axis=0, concat_axis=0, tiled=True)
    results = results.reshape(experts * capacity, width)
    return jnp.dot(combine_map, results, preferred_element_type=jnp.float32).astype(jnp.bfloat16)


def solution(mesh):
    return jax.shard_map(
        on_device,
        mesh=mesh,
        in_specs=(
            P(("dp", "node", "chip"), None),
            P(("dp", "node", "chip"), None),
            P(("dp", "node", "chip"), None),
            P(("node", "chip"), None, None),
            P(("node", "chip"), None, None),
            P(("node", "chip"), None, None),
        ),
        out_specs=P(("dp", "node", "chip"), None),
        check_vma=False,
    )
```

profile of v0, /device:TPU:710, one launch (start us, length us, event | category | flops | bytes accessed | tf_op | source)
XLA Modules:
  0.0 137.1 jit_solution(13542167715822151486)
XLA Ops:
  0.0 0.0 copy-start
  0.0 0.9 copy.17
  0.9 0.1 eq.44
  1.0 0.1 eq.40
  1.1 0.7 broadcast_multiply_fusion
  1.8 1.2 reduce-window.6
  3.0 0.2 slice_reduce_fusion
  3.2 0.1 fusion.17
  3.4 0.1 reduce_sum.21
  3.4 0.1 copy.20
  3.6 0.4 fusion.12
  4.0 1.7 %convolution_convert_fusion = bf16[512,2048]{1,0:T(8,128)(2,1)S(1)} fusion(pred[64,512]{1,0:T(8,128)(4,1)S(1)} %fusion.12, bf16[64,2048]{1,0:T(8,128)(2,1)} %param.6), kind=kOutput, calls=%fused_computation.7 | convolution fusion | flops 135266304 | bytes 2392064 | tf_op jit(solution)/shard_map/dot_general | solution.py:43
  5.7 0.0 copy-start.3
  5.7 60.8 %all_to_all.10 = bf16[32,16,2048]{2,1,0:T(8,128)(2,1)S(1)} all-to-all(bf16[32,16,2048]{2,1,0:T(8,128)(2,1)S(1)} %bitcast.44), channel_id=1, replica_groups=mesh['dp'=24,'node'=8,'chip'=4] {'node','chip'}, dimensions={0} | all-to-all | bytes 4194304 | tf_op jit(solution)/shard_map/all_to_all | solution.py:48
  66.5 1.3 copy-done.1
  67.8 0.0 copy-done.3
  67.8 3.0 %fusion.4 = f32[512,768]{1,0:T(8,128)} fusion(bf16[512,2048]{1,0:T(8,128)(2,1)S(1)} %bitcast.46, bf16[1,2048,768]{2,1,0:T(8,128)(2,1)S(1)} %copy-done.3), kind=kOutput, calls=%fused_computation.4 | convolution fusion | flops 1610612736 | bytes 6815744 | tf_op jit(solution)/shard_map/dot_general | solution.py:29
  70.8 0.0 copy-done
  70.8 8.3 %fusion.6 = bf16[512,2048]{1,0:T(8,128)(2,1)} fusion(bf16[1,768,2048]{2,1,0:T(8,128)(2,1)S(1)} %copy-done, f32[512,768]{1,0:T(8,128)} %fusion.4, bf16[512,2048]{1,0:T(8,128)(2,1)} %bitcast.47, bf16[1,2048,768]{2,1,0:T(8,128)(2,1)} %param.10), kind=kOutput, calls=%fused_computation.6 | convolution fusion | flops 3224633344 | bytes 12058624 | tf_op jit(solution)/shard_map/dot_general | solution.py:32
  79.1 5.8 %all-to-all-start.1 = ((bf16[32,16,2048]{2,1,0:T(8,128)(2,1)}), bf16[32,16,2048]{2,1,0:T(8,128)(2,1)}, u32[]{:S(2)}, u32[]{:S(2)}) async-start(bf16[32,16,2048]{2,1,0:T(8,128)(2,1)} %bitcast.45), calls=%async_computation.1 | async-start | bytes 4194304 | tf_op jit(solution)/shard_map/all_to_all | solution.py:53
  84.9 0.1 copy.21
  84.9 0.5 select_reduce_fusion
  85.4 48.9 %all-to-all-done.1 = bf16[32,16,2048]{2,1,0:T(8,128)(2,1)} async-done(((bf16[32,16,2048]{2,1,0:T(8,128)(2,1)}), bf16[32,16,2048]{2,1,0:T(8,128)(2,1)}, u32[]{:S(2)}, u32[]{:S(2)}) %all-to-all-start.1) | async-done | bytes 2097184 | tf_op jit(solution)/shard_map/all_to_all | solution.py:53
  134.4 2.8 %convolution_convert_fusion.1 = bf16[64,2048]{1,0:T(8,128)(2,1)} fusion(bf16[512,2048]{1,0:T(8,128)(2,1)} %bitcast.7, bf16[64,512]{1,0:T(8,128)(2,1)S(1)} %select_reduce_fusion), kind=kOutput, calls=%fused_computation.8 | convolution fusion | flops 134348800 | bytes 2424832 | tf_op jit(solution)/shard_map/dot_general | solution.py:55
  (9 shorter events, 0.1 us)
Async XLA Ops:
  0.0 70.8 %copy-start = (bf16[1,768,2048]{2,1,0:T(8,128)(2,1)S(1)}, bf16[1,768,2048]{2,1,0:T(8,128)(2,1)}, u32[]{:S(2)}) copy-start(bf16[1,768,2048]{2,1,0:T(8,128)(2,1)} %param.11) | copy-start | bytes 9437188
  5.7 62.1 %copy-start.3 = (bf16[1,2048,768]{2,1,0:T(8,128)(2,1)S(1)}, bf16[1,2048,768]{2,1,0:T(8,128)(2,1)}, u32[]{:S(2)}) copy-start(bf16[1,2048,768]{2,1,0:T(8,128)(2,1)} %param.9) | copy-start | bytes 9437188
  66.5 1.3 copy-start.1
  79.1 5.8 %copy-start.2 = (s32[64,8]{0,1:T(8,128)S(1)}, s32[64,8]{0,1:T(8,128)}, u32[]{:S(2)}) copy-start(s32[64,8]{0,1:T(8,128)} %param.8) | copy-start | bytes 6148
  79.1 55.3 %all-to-all-start.1 = ((bf16[32,16,2048]{2,1,0:T(8,128)(2,1)}), bf16[32,16,2048]{2,1,0:T(8,128)(2,1)}, u32[]{:S(2)}, u32[]{:S(2)}) async-start(bf16[32,16,2048]{2,1,0:T(8,128)(2,1)} %bitcast.45), calls=%async_computation.1 | async-start | bytes 4194304 | tf_op jit(solution)/shard_map/all_to_all | solution.py:53
where the time goes:
time: 137 us
  blocking collectives  60.8 us (44%)
  waiting for transfers between devices  48.9 us (36%)
  matrix products  15.7 us (11%)
  starting transfers between devices  5.75 us (4%)
  other arithmetic  2.97 us (2%)
  local copies, waits for them, and re-layouts  2.89 us (2%)
    all_to_all x1, blocking collectives, on_device(): lax.all_to_all(outbound, ('node', 'chip'), split_axis=0, concat_axis=0, t...  60.8 us
    all_to_all x1, waiting for transfers between devices, on_device(): lax.all_to_all(served, ('node', 'chip'), split_axis=0, concat_axis=0, til...  48.9 us
    dot_general x1, matrix products, expert_ffn(): jnp.dot(hidden, down_mat, preferred_element_type=jnp.float32)  8.28 us
    all_to_all x1, starting transfers between devices, on_device(): lax.all_to_all(served, ('node', 'chip'), split_axis=0, concat_axis=0, til...  5.75 us
    dot_general x1, matrix products, expert_ffn(): gate_act = jnp.dot(row_block, gate_mat, preferred_element_type=jnp.float32)  2.97 us
    dot_general x1, matrix products, on_device(): jnp.dot(combine_map, results, preferred_element_type=jnp.float32)  2.78 us
  transfers between devices with their start and end apart: 1, of which 1 were waited for; matrix products, arithmetic and copies ran while one was open for 0% of the time, Pallas kernels for 0%

commit v1 on v0

v1 whole, which is shorter than its diff:
```python
import jax
import jax.numpy as jnp
from jax import lax
from jax.experimental import pallas as pl
from jax.experimental.pallas import tpu as pltpu
from jax.sharding import PartitionSpec as P

SPLIT = (8, 8)


def tables_kernel(split, experts, ids_ref, gates_ref, tokens_ref, *out_refs):
    rows_refs, maps_refs = out_refs[: len(split)], out_refs[len(split) :]
    tok_dev, top_count = ids_ref.shape
    ids, gates = ids_ref[...], gates_ref[...]
    expert = lax.broadcasted_iota(jnp.int32, (tok_dev, experts), 1)
    named = jnp.zeros((tok_dev, experts), jnp.float32)
    weight = jnp.zeros((tok_dev, experts), jnp.float32)
    for k in range(top_count):
        hit = ids[:, k : k + 1] == expert
        named = jnp.where(hit, 1.0, named)
        weight = jnp.where(hit, gates[:, k : k + 1].astype(jnp.float32), weight)
    earlier = lax.broadcasted_iota(jnp.int32, (tok_dev, tok_dev), 1) < lax.broadcasted_iota(
        jnp.int32, (tok_dev, tok_dev), 0
    )
    rank = jnp.dot(
        jnp.where(earlier, 1.0, 0.0).astype(jnp.bfloat16),
        named.astype(jnp.bfloat16),
        preferred_element_type=jnp.float32,
    )
    rank = jnp.where(named > 0.0, rank, -1.0).astype(jnp.bfloat16)
    weight = weight.astype(jnp.bfloat16)
    tokens = tokens_ref[...]
    first = 0
    for size, rows_ref, map_ref in zip(split, rows_refs, maps_refs):
        slots = experts * size
        row = lax.broadcasted_iota(jnp.int32, (experts, slots), 1)
        spread = jnp.where(
            row // size == lax.broadcasted_iota(jnp.int32, (experts, slots), 0), 1.0, 0.0
        ).astype(jnp.bfloat16)
        slot = lax.broadcasted_iota(jnp.int32, (tok_dev, slots), 1) % size + first
        placed = jnp.dot(rank, spread, preferred_element_type=jnp.float32) == slot.astype(
            jnp.float32
        )
        share = jnp.dot(weight, spread, preferred_element_type=jnp.float32) * (1.0 / 256.0)
        map_ref[...] = jnp.where(placed, share, 0.0).astype(map_ref.dtype)
        rows_ref[...] = lax.dot_general(
            jnp.where(placed, 1.0, 0.0).astype(jnp.bfloat16),
            tokens,
            (((0,), (0,)), ((), ())),
            preferred_element_type=jnp.float32,
        ).astype(rows_ref.dtype)
        first += size


def build_tables(ids, gates, tokens, experts, split):
    tok_dev, width = tokens.shape
    shapes = [jax.ShapeDtypeStruct((experts * s, width), jnp.bfloat16) for s in split] + [
        jax.ShapeDtypeStruct((tok_dev, experts * s), jnp.bfloat16) for s in split
    ]
    whole = pl.BlockSpec(memory_space=pltpu.VMEM)
    outs = pl.pallas_call(
        lambda *refs: tables_kernel(split, experts, *refs),
        out_shape=shapes,
        in_specs=[whole] * 3,
        out_specs=[whole] * len(shapes),
        compiler_params=pltpu.CompilerParams(vmem_limit_bytes=24 * 1024 * 1024),
        name="tables",
    )(ids, gates, tokens)
    return outs[: len(split)], outs[len(split) :]


def expert_ffn(arrived, gate_mat, up_mat, down_mat):
    width = arrived.shape[-1]
    row_block = arrived.reshape(-1, width)
    gate_act = jnp.dot(row_block, gate_mat, preferred_element_type=jnp.float32)
    up_act = jnp.dot(row_block, up_mat, preferred_element_type=jnp.float32)
    hidden = (jax.nn.silu(gate_act) * up_act).astype(jnp.bfloat16)
    output = jnp.dot(hidden, down_mat, preferred_element_type=jnp.float32).astype(jnp.bfloat16)
    return output.reshape(arrived.shape)


def on_device(tokens, expert_ids, gate_fixed, w_gate, w_up, w_down):
    width = tokens.shape[1]
    experts = lax.axis_size(("node", "chip")) * w_gate.shape[0]
    outbound, maps = build_tables(expert_ids, gate_fixed, tokens, experts, SPLIT)

    def exchange(block):
        return lax.all_to_all(block, ("node", "chip"), split_axis=0, concat_axis=0, tiled=True)

    arrived = [exchange(rows.reshape(experts, -1, width)) for rows in outbound]
    served = [expert_ffn(block, w_gate[0], w_up[0], w_down[0]) for block in arrived]
    results = [exchange(block) for block in served]
    total = 0.0
    for combine_map, result in zip(maps, results):
        total = total + jnp.dot(
            combine_map, result.reshape(-1, width), preferred_element_type=jnp.float32
        )
    return total.astype(jnp.bfloat16)


def solution(mesh):
    return jax.shard_map(
        on_device,
        mesh=mesh,
        in_specs=(
            P(("dp", "node", "chip"), None),
            P(("dp", "node", "chip"), None),
            P(("dp", "node", "chip"), None),
            P(("node", "chip"), None, None),
            P(("node", "chip"), None, None),
            P(("node", "chip"), None, None),
        ),
        out_specs=P(("dp", "node", "chip"), None),
        check_vma=False,
    )
```

time: 137 us -> 142 us (1.036)
  the two profiles are of different devices: /device:TPU:710 before, /device:TPU:514 now
where the time goes in v1:
time: 142 us; the launch traced here: 141 us
  waiting for transfers between devices  58.4 us (41%)
  blocking collectives  38.2 us (27%)
  matrix products  23.9 us (17%)
  starting transfers between devices  16.9 us (12%)
  local copies, waits for them, and re-layouts  2.69 us (2%)
    all_to_all x3, waiting for transfers between devices, exchange(): lax.all_to_all(block, ('node', 'chip'), split_axis=0, concat_axis=0, tile...  58.4 us
    all_to_all x1, blocking collectives, exchange(): lax.all_to_all(block, ('node', 'chip'), split_axis=0, concat_axis=0, tile...  38.2 us
    all_to_all x3, starting transfers between devices, exchange(): lax.all_to_all(block, ('node', 'chip'), split_axis=0, concat_axis=0, tile...  16.9 us
    dot_general x2, matrix products, expert_ffn(): jnp.dot(hidden, down_mat, preferred_element_type=jnp.float32)  11.1 us
    dot_general x2, matrix products, expert_ffn(): gate_act = jnp.dot(row_block, gate_mat, preferred_element_type=jnp.float32)  8.15 us
    dot_general x2, matrix products, on_device(): jnp.dot(combine_map, result.reshape(-1, width), preferred_element_type=jn...  4.71 us
  transfers between devices with their start and end apart: 3, of which 3 were waited for; matrix products, arithmetic and copies ran while one was open for 15% of the time, Pallas kernels for 0%

profile of v1, /device:TPU:514, one launch (start us, length us, event | category | flops | bytes accessed | tf_op | source)
XLA Modules:
  0.0 141.3 jit_solution(14304414513865879959)
XLA Ops:
  0.0 0.0 copy-start
  0.0 0.9 copy.7.refs_0_
  0.9 0.8 copy.8.refs_1_
  1.7 0.0 copy-start.2
  1.7 0.9 copy-done.2
  2.7 1.1 tables.1
  3.8 0.0 copy-start.1
  3.8 38.2 %all_to_all.20 = bf16[32,8,2048]{2,1,0:T(8,128)(2,1)} all-to-all(bf16[32,8,2048]{2,1,0:T(8,128)(2,1)S(1)} %bitcast.64), channel_id=1, replica_groups=mesh['dp'=24,'node'=8,'chip'=4] {'node','chip'}, dimensions={0} | all-to-all | bytes 2097152 | tf_op jit(solution)/shard_map/all_to_all | solution.py:88
  42.1 0.0 copy-done.1
  42.1 5.6 %all-to-all-start.2 = ((bf16[32,8,2048]{2,1,0:T(8,128)(2,1)}), bf16[32,8,2048]{2,1,0:T(8,128)(2,1)}, u32[]{:S(2)}, u32[]{:S(2)}) async-start(bf16[32,8,2048]{2,1,0:T(8,128)(2,1)} %bitcast.63), calls=%async_computation.2 | async-start | bytes 2097152 | tf_op jit(solution)/shard_map/all_to_all | solution.py:88
  47.7 4.1 %fusion.10 = f32[256,768]{1,0:T(8,128)} fusion(bf16[1,2048,768]{2,1,0:T(8,128)(2,1)} %param.9, bf16[32,8,2048]{2,1,0:T(8,128)(2,1)} %all_to_all.20), kind=kOutput, calls=%fused_computation.10 | convolution fusion | flops 805306368 | bytes 4980736 | tf_op jit(solution)/shard_map/dot_general | solution.py:75
  51.8 0.0 copy-done
  51.8 5.5 %fusion.21 = bf16[32,8,2048]{2,1,0:T(8,128)(2,1)} fusion(bf16[1,768,2048]{2,1,0:T(8,128)(2,1)S(1)} %copy-done, bf16[1,2048,768]{2,1,0:T(8,128)(2,1)} %param.10, bf16[32,8,2048]{2,1,0:T(8,128)(2,1)} %all_to_all.20, f32[256,768]{1,0:T(8,128)} %fusion.10), kind=kOutput, calls=%fused_computation.15 | convolution fusion | flops 1612316672 | bytes 9175040 | tf_op jit(solution)/shard_map/dot_general | solution.py:78
  57.3 17.4 %all-to-all-done.2 = bf16[32,8,2048]{2,1,0:T(8,128)(2,1)} async-done(((bf16[32,8,2048]{2,1,0:T(8,128)(2,1)}), bf16[32,8,2048]{2,1,0:T(8,128)(2,1)}, u32[]{:S(2)}, u32[]{:S(2)}) %all-to-all-start.2) | async-done | bytes 1048608 | tf_op jit(solution)/shard_map/all_to_all | solution.py:88
  74.7 5.6 %all-to-all-start.1 = ((bf16[32,8,2048]{2,1,0:T(8,128)(2,1)}), bf16[32,8,2048]{2,1,0:T(8,128)(2,1)}, u32[]{:S(2)}, u32[]{:S(2)}) async-start(bf16[32,8,2048]{2,1,0:T(8,128)(2,1)} %fusion.21), calls=%async_computation.1 | async-start | bytes 2097152 | tf_op jit(solution)/shard_map/all_to_all | solution.py:88
  80.4 4.1 %fusion.8 = f32[256,768]{1,0:T(8,128)} fusion(bf16[1,2048,768]{2,1,0:T(8,128)(2,1)} %param.9, bf16[32,8,2048]{2,1,0:T(8,128)(2,1)} %all-to-all-done.2), kind=kOutput, calls=%fused_computation.8 | convolution fusion | flops 805306368 | bytes 4980736 | tf_op jit(solution)/shard_map/dot_general | solution.py:75
  84.5 5.5 %fusion.18 = bf16[32,8,2048]{2,1,0:T(8,128)(2,1)} fusion(bf16[1,768,2048]{2,1,0:T(8,128)(2,1)S(1)} %copy-done, bf16[1,2048,768]{2,1,0:T(8,128)(2,1)} %param.10, bf16[32,8,2048]{2,1,0:T(8,128)(2,1)} %all-to-all-done.2, f32[256,768]{1,0:T(8,128)} %fusion.8), kind=kOutput, calls=%fused_computation.14 | convolution fusion | flops 1612316672 | bytes 9175040 | tf_op jit(solution)/shard_map/dot_general | solution.py:78
  90.0 17.0 %all-to-all-done.1 = bf16[32,8,2048]{2,1,0:T(8,128)(2,1)} async-done(((bf16[32,8,2048]{2,1,0:T(8,128)(2,1)}), bf16[32,8,2048]{2,1,0:T(8,128)(2,1)}, u32[]{:S(2)}, u32[]{:S(2)}) %all-to-all-start.1) | async-done | bytes 1048608 | tf_op jit(solution)/shard_map/all_to_all | solution.py:88
  107.0 5.6 %all-to-all-start.3 = ((bf16[32,8,2048]{2,1,0:T(8,128)(2,1)}), bf16[32,8,2048]{2,1,0:T(8,128)(2,1)}, u32[]{:S(2)}, u32[]{:S(2)}) async-start(bf16[32,8,2048]{2,1,0:T(8,128)(2,1)} %fusion.18), calls=%async_computation.3 | async-start | bytes 2097152 | tf_op jit(solution)/shard_map/all_to_all | solution.py:88
  112.6 2.3 %fusion.40 = f32[64,2048]{1,0:T(8,128)} fusion(bf16[64,256]{1,0:T(8,128)(2,1)S(1)} %get-tuple-element.9, bf16[32,8,2048]{2,1,0:T(8,128)(2,1)} %all-to-all-done.1), kind=kOutput, calls=%fused_computation.25 | convolution fusion | flops 67108864 | bytes 1605632 | tf_op jit(solution)/shard_map/dot_general | solution.py:95
  115.0 24.0 %all-to-all-done.3 = bf16[32,8,2048]{2,1,0:T(8,128)(2,1)} async-done(((bf16[32,8,2048]{2,1,0:T(8,128)(2,1)}), bf16[32,8,2048]{2,1,0:T(8,128)(2,1)}, u32[]{:S(2)}, u32[]{:S(2)}) %all-to-all-start.3) | async-done | bytes 1048608 | tf_op jit(solution)/shard_map/all_to_all | solution.py:88
  138.9 2.4 %fusion.24 = bf16[64,2048]{1,0:T(8,128)(2,1)} fusion(f32[64,2048]{1,0:T(8,128)} %fusion.40, bf16[64,256]{1,0:T(8,128)(2,1)S(1)} %get-tuple-element.11, bf16[32,8,2048]{2,1,0:T(8,128)(2,1)} %all-to-all-done.3), kind=kOutput, calls=%fused_computation.17 | convolution fusion | flops 67371008 | bytes 1867776 | tf_op jit(solution)/shard_map/dot_general | solution.py:95
Async XLA Ops:
  0.0 51.8 %copy-start = (bf16[1,768,2048]{2,1,0:T(8,128)(2,1)S(1)}, bf16[1,768,2048]{2,1,0:T(8,128)(2,1)}, u32[]{:S(2)}) copy-start(bf16[1,768,2048]{2,1,0:T(8,128)(2,1)} %param.11) | copy-start | bytes 9437188
  1.7 0.9 copy-start.2
  3.8 38.2 %copy-start.1 = (bf16[256,2048]{1,0:T(8,128)(2,1)}, bf16[256,2048]{1,0:T(8,128)(2,1)S(1)}, u32[]{:S(2)}) copy-start(bf16[256,2048]{1,0:T(8,128)(2,1)S(1)} %get-tuple-element.12) | copy-start | bytes 3145732
  42.1 32.7 %all-to-all-start.2 = ((bf16[32,8,2048]{2,1,0:T(8,128)(2,1)}), bf16[32,8,2048]{2,1,0:T(8,128)(2,1)}, u32[]{:S(2)}, u32[]{:S(2)}) async-start(bf16[32,8,2048]{2,1,0:T(8,128)(2,1)} %bitcast.63), calls=%async_computation.2 | async-start | bytes 2097152 | tf_op jit(solution)/shard_map/all_to_all | solution.py:88
  74.7 32.2 %all-to-all-start.1 = ((bf16[32,8,2048]{2,1,0:T(8,128)(2,1)}), bf16[32,8,2048]{2,1,0:T(8,128)(2,1)}, u32[]{:S(2)}, u32[]{:S(2)}) async-start(bf16[32,8,2048]{2,1,0:T(8,128)(2,1)} %fusion.21), calls=%async_computation.1 | async-start | bytes 2097152 | tf_op jit(solution)/shard_map/all_to_all | solution.py:88
  107.0 31.9 %all-to-all-start.3 = ((bf16[32,8,2048]{2,1,0:T(8,128)(2,1)}), bf16[32,8,2048]{2,1,0:T(8,128)(2,1)}, u32[]{:S(2)}, u32[]{:S(2)}) async-start(bf16[32,8,2048]{2,1,0:T(8,128)(2,1)} %fusion.18), calls=%async_computation.3 | async-start | bytes 2097152 | tf_op jit(solution)/shard_map/all_to_all | solution.py:88

commit v2 on v0

v2 whole, which is shorter than its diff:
```python
import jax
import jax.numpy as jnp
from jax import lax
from jax.experimental import pallas as pl
from jax.experimental.pallas import tpu as pltpu
from jax.sharding import PartitionSpec as P

MIB = 1024 * 1024


def tables_kernel(experts, ids_ref, gates_ref, tokens_ref, rows_ref, map_ref, tokens, arrived):
    fetch = pltpu.make_async_copy(tokens_ref, tokens, arrived)
    fetch.start()
    top_count, tok_dev = ids_ref.shape
    slots = rows_ref.shape[0]
    capacity = slots // experts
    ids, gates = ids_ref[...], gates_ref[...].astype(jnp.float32)
    expert = lax.broadcasted_iota(jnp.int32, (experts, tok_dev), 0)
    named = jnp.zeros((experts, tok_dev), jnp.float32)
    weight = jnp.zeros((experts, tok_dev), jnp.float32)
    for k in range(top_count):
        hit = ids[k : k + 1, :] == expert
        named = jnp.where(hit, 1.0, named)
        weight = jnp.where(hit, gates[k : k + 1, :], weight)
    earlier = lax.broadcasted_iota(jnp.int32, (tok_dev, tok_dev), 0) < lax.broadcasted_iota(
        jnp.int32, (tok_dev, tok_dev), 1
    )
    rank = jnp.dot(
        named.astype(jnp.bfloat16),
        jnp.where(earlier, 1.0, 0.0).astype(jnp.bfloat16),
        preferred_element_type=jnp.float32,
    )
    rank = jnp.where(named > 0.0, rank, -1.0).astype(jnp.bfloat16)
    row = lax.broadcasted_iota(jnp.int32, (slots, experts), 0)
    spread = jnp.where(
        row // capacity == lax.broadcasted_iota(jnp.int32, (slots, experts), 1), 1.0, 0.0
    ).astype(jnp.bfloat16)
    slot = lax.broadcasted_iota(jnp.int32, (slots, tok_dev), 0) % capacity
    placed = jnp.dot(spread, rank, preferred_element_type=jnp.float32) == slot.astype(
        jnp.float32
    )
    share = jnp.dot(spread, weight.astype(jnp.bfloat16), preferred_element_type=jnp.float32)
    map_ref[...] = jnp.where(placed, share * (1.0 / 256.0), 0.0).astype(map_ref.dtype)
    chosen = jnp.where(placed, 1.0, 0.0).astype(jnp.bfloat16)
    fetch.wait()
    rows_ref[...] = jnp.dot(chosen, tokens[...], preferred_element_type=jnp.float32).astype(
        rows_ref.dtype
    )


def build_tables(ids, gates, tokens, experts, capacity):
    tok_dev, width = tokens.shape
    whole = pl.BlockSpec(memory_space=pltpu.VMEM)
    return pl.pallas_call(
        lambda *refs: tables_kernel(experts, *refs),
        out_shape=(
            jax.ShapeDtypeStruct((experts * capacity, width), jnp.bfloat16),
            jax.ShapeDtypeStruct((experts * capacity, tok_dev), jnp.bfloat16),
        ),
        in_specs=[whole, whole, pl.BlockSpec(memory_space=pl.ANY)],
        out_specs=(whole, whole),
        scratch_shapes=[
            pltpu.VMEM((tok_dev, width), jnp.bfloat16),
            pltpu.SemaphoreType.DMA,
        ],
        compiler_params=pltpu.CompilerParams(vmem_limit_bytes=24 * MIB),
        name="tables",
    )(ids.T, gates.T, tokens)


def ffn_kernel(step, rows_ref, gate_ref, up_ref, down_ref, out_ref, up, down, gated, hidden, arrived):
    fetch_up = pltpu.make_async_copy(up_ref, up, arrived.at[0])
    fetch_down = pltpu.make_async_copy(down_ref, down, arrived.at[1])
    fetch_up.start()
    fetch_down.start()
    rows = rows_ref[...]
    for at in range(0, gate_ref.shape[1], step):
        part = pl.ds(at, step)
        gate_act = jnp.dot(rows, gate_ref[:, part], preferred_element_type=jnp.float32)
        gated[:, part] = gate_act / (1.0 + jnp.exp(-gate_act))
    fetch_up.wait()
    for at in range(0, gate_ref.shape[1], step):
        part = pl.ds(at, step)
        up_act = jnp.dot(rows, up[:, part], preferred_element_type=jnp.float32)
        hidden[:, part] = (gated[:, part] * up_act).astype(hidden.dtype)
    fetch_down.wait()
    for at in range(0, down.shape[1], step):
        part = pl.ds(at, step)
        out_ref[:, part] = jnp.dot(
            hidden[...], down[:, part], preferred_element_type=jnp.float32
        ).astype(out_ref.dtype)


def expert_ffn(rows, gate_mat, up_mat, down_mat):
    count, width = rows.shape
    ff = gate_mat.shape[1]
    whole = pl.BlockSpec(memory_space=pltpu.VMEM)
    away = pl.BlockSpec(memory_space=pl.ANY)
    return pl.pallas_call(
        lambda *refs: ffn_kernel(256, *refs),
        out_shape=jax.ShapeDtypeStruct((count, width), jnp.bfloat16),
        in_specs=[whole, whole, away, away],
        out_specs=whole,
        scratch_shapes=[
            pltpu.VMEM((width, ff), jnp.bfloat16),
            pltpu.VMEM((ff, width), jnp.bfloat16),
            pltpu.VMEM((count, ff), jnp.float32),
            pltpu.VMEM((count, ff), jnp.bfloat16),
            pltpu.SemaphoreType.DMA((2,)),
        ],
        compiler_params=pltpu.CompilerParams(vmem_limit_bytes=32 * MIB),
        cost_estimate=pl.CostEstimate(
            flops=6 * count * width * ff,
            bytes_accessed=6 * width * ff + 4 * count * width,
            transcendentals=count * ff,
        ),
        name="ffn",
    )(rows, gate_mat, up_mat, down_mat)


def combine_kernel(map_ref, results_ref, out_ref):
    out_ref[...] = lax.dot_general(
        map_ref[...],
        results_ref[...],
        (((0,), (0,)), ((), ())),
        preferred_element_type=jnp.float32,
    ).astype(out_ref.dtype)


def combine(combine_map, results, step=512):
    slots, width = results.shape
    tok_dev = combine_map.shape[1]
    return pl.pallas_call(
        combine_kernel,
        out_shape=jax.ShapeDtypeStruct((tok_dev, width), jnp.bfloat16),
        grid=(width // step,),
        in_specs=[
            pl.BlockSpec((slots, tok_dev), lambda i: (0, 0)),
            pl.BlockSpec((slots, step), lambda i: (0, i)),
        ],
        out_specs=pl.BlockSpec((tok_dev, step), lambda i: (0, i)),
        compiler_params=pltpu.CompilerParams(vmem_limit_bytes=16 * MIB),
        name="combine",
    )(combine_map, results)


def on_device(tokens, expert_ids, gate_fixed, w_gate, w_up, w_down):
    tok_dev, width = tokens.shape
    top_count = expert_ids.shape[1]
    experts = lax.axis_size(("node", "chip")) * w_gate.shape[0]
    capacity = tok_dev * top_count // experts
    outbound, combine_map = build_tables(expert_ids, gate_fixed, tokens, experts, capacity)

    def exchange(rows):
        blocks = rows.reshape(experts, capacity, width)
        return lax.all_to_all(
            blocks, ("node", "chip"), split_axis=0, concat_axis=0, tiled=True
        ).reshape(experts * capacity, width)

    served = expert_ffn(exchange(outbound), w_gate[0], w_up[0], w_down[0])
    return combine(combine_map, exchange(served))


def solution(mesh):
    return jax.shard_map(
        on_device,
        mesh=mesh,
        in_specs=(
            P(("dp", "node", "chip"), None),
            P(("dp", "node", "chip"), None),
            P(("dp", "node", "chip"), None),
            P(("node", "chip"), None, None),
            P(("node", "chip"), None, None),
            P(("node", "chip"), None, None),
        ),
        out_specs=P(("dp", "node", "chip"), None),
        check_vma=False,
    )
```

time: 137 us -> 132 us (0.964)
  the two profiles are of different devices: /device:TPU:710 before, /device:TPU:706 now
where the time goes in v2:
time: 132 us
  blocking collectives  116 us (88%)
  Pallas kernels  10 us (8%)
  local copies, waits for them, and re-layouts  6.11 us (5%)
    all_to_all x2, blocking collectives, exchange(): lax.all_to_all(blocks, ('node', 'chip'), split_axis=0, concat_axis=0, til...  116 us
    pallas_call x1, Pallas kernels, expert_ffn(): pl.pallas_call(lambda *refs: ffn_kernel(256, *refs), out_shape=jax.ShapeD...  6.89 us
    unnamed x12, local copies, waits for them, and re-layouts  6.11 us

profile of v2, /device:TPU:706, one launch (start us, length us, event | category | flops | bytes accessed | tf_op | source)
XLA Modules:
  0.0 131.8 jit_solution(2561508174046699966)
XLA Ops:
  0.0 0.0 copy-start
  0.0 0.9 copy-done
  1.0 0.0 copy-start.1
  1.0 0.7 copy-done.1
  1.6 0.0 copy-start.2
  1.6 0.7 copy-done.2
  2.3 1.0 tables.1
  3.4 0.0 copy-start.3
  3.4 60.9 %all_to_all.10 = bf16[32,16,2048]{2,1,0:T(8,128)(2,1)S(1)} all-to-all(bf16[32,16,2048]{2,1,0:T(8,128)(2,1)S(1)} %bitcast.10), channel_id=1, replica_groups=mesh['dp'=24,'node'=8,'chip'=4] {'node','chip'}, dimensions={0} | all-to-all | bytes 4194304 | tf_op jit(solution)/shard_map/all_to_all | solution.py:156
  64.2 0.0 copy-done.3
  64.2 0.0 copy-start.4
  64.2 1.9 %copy-done.4 = bf16[1,2048,768]{2,1,0:T(8,128)(2,1)S(1)} copy-done((bf16[1,2048,768]{2,1,0:T(8,128)(2,1)S(1)}, bf16[1,2048,768]{2,1,0:T(8,128)(2,1)}, u32[]{:S(2)}) %copy-start.4) | copy-done | bytes 3145752
  66.1 0.0 copy-start.5
  66.1 1.9 %copy-done.5 = bf16[1,768,2048]{2,1,0:T(8,128)(2,1)S(1)} copy-done((bf16[1,768,2048]{2,1,0:T(8,128)(2,1)S(1)}, bf16[1,768,2048]{2,1,0:T(8,128)(2,1)}, u32[]{:S(2)}) %copy-start.5) | copy-done | bytes 3145752
  68.0 6.9 %ffn.1 = bf16[512,2048]{1,0:T(8,128)(2,1)S(1)} custom-call(bf16[512,2048]{1,0:T(8,128)(2,1)S(1)} %bitcast.11, bf16[2048,768]{1,0:T(8,128)(2,1)S(1)} %bitcast.15, bf16[2048,768]{1,0:T(8,128)(2,1)S(1)} %bitcast.16, bf16[768,2048]{1,0:T(8,128)(2,1)S(1)} %bitcast.17), custom_call_target="tpu_custom_call" | custom-call | flops 4831838208 | bytes 13631488 | tf_op jit(solution)/shard_map/ffn/pallas_call | solution.py:99
  74.9 54.8 %all_to_all.11 = bf16[32,16,2048]{2,1,0:T(8,128)(2,1)S(1)} all-to-all(bf16[32,16,2048]{2,1,0:T(8,128)(2,1)S(1)} %bitcast.12), channel_id=1, replica_groups=mesh['dp'=24,'node'=8,'chip'=4] {'node','chip'}, dimensions={0} | all-to-all | bytes 4194304 | tf_op jit(solution)/shard_map/all_to_all | solution.py:156
  129.8 2.1 %combine.1 = bf16[64,2048]{1,0:T(8,128)(2,1)} custom-call(bf16[512,64]{1,0:T(8,128)(2,1)S(1)} %get-tuple-element.7.map_ref, bf16[512,2048]{1,0:T(8,128)(2,1)S(1)} %bitcast.9), custom_call_target="tpu_custom_call" | custom-call | tf_op jit(solution)/shard_map/combine/pallas_call | solution.py:133
Async XLA Ops:
  0.0 0.9 copy-start
  1.0 0.7 copy-start.1
  1.6 0.7 copy-start.2
  3.4 60.9 %copy-start.3 = (bf16[1,2048,768]{2,1,0:T(8,128)(2,1)S(1)}, bf16[1,2048,768]{2,1,0:T(8,128)(2,1)}, u32[]{:S(2)}) copy-start(bf16[1,2048,768]{2,1,0:T(8,128)(2,1)} %param.9) | copy-start | bytes 9437188
  64.2 1.9 %copy-start.4 = (bf16[1,2048,768]{2,1,0:T(8,128)(2,1)S(1)}, bf16[1,2048,768]{2,1,0:T(8,128)(2,1)}, u32[]{:S(2)}) copy-start(bf16[1,2048,768]{2,1,0:T(8,128)(2,1)} %param.10) | copy-start | bytes 9437188
  66.1 1.9 %copy-start.5 = (bf16[1,768,2048]{2,1,0:T(8,128)(2,1)S(1)}, bf16[1,768,2048]{2,1,0:T(8,128)(2,1)}, u32[]{:S(2)}) copy-start(bf16[1,768,2048]{2,1,0:T(8,128)(2,1)} %param.11) | copy-start | bytes 9437188

commit v3 on v2

--- a/solution.py
+++ b/solution.py
@@ -8,13 +8,32 @@
 MIB = 1024 * 1024
 
 
-def tables_kernel(experts, ids_ref, gates_ref, tokens_ref, rows_ref, map_ref, tokens, arrived):
-    fetch = pltpu.make_async_copy(tokens_ref, tokens, arrived)
-    fetch.start()
+def tables_kernel(
+    experts,
+    ids_ref,
+    gates_ref,
+    tokens_ref,
+    rows_ref,
+    map_ref,
+    ids_here,
+    gates_here,
+    tokens,
+    rows,
+    arrived,
+    left,
+):
+    fetch_ids = pltpu.make_async_copy(ids_ref, ids_here, arrived.at[0])
+    fetch_gates = pltpu.make_async_copy(gates_ref, gates_here, arrived.at[1])
+    fetch_tokens = pltpu.make_async_copy(tokens_ref, tokens, arrived.at[2])
+    fetch_ids.start()
+    fetch_gates.start()
+    fetch_tokens.start()
     top_count, tok_dev = ids_ref.shape
     slots = rows_ref.shape[0]
     capacity = slots // experts
-    ids, gates = ids_ref[...], gates_ref[...].astype(jnp.float32)
+    fetch_ids.wait()
+    fetch_gates.wait()
+    ids, gates = ids_here[...], gates_here[...].astype(jnp.float32)
     expert = lax.broadcasted_iota(jnp.int32, (experts, tok_dev), 0)
     named = jnp.zeros((experts, tok_dev), jnp.float32)
     weight = jnp.zeros((experts, tok_dev), jnp.float32)
@@ -42,10 +61,18 @@
     share = jnp.dot(spread, weight.astype(jnp.bfloat16), preferred_element_type=jnp.float32)
     map_ref[...] = jnp.where(placed, share * (1.0 / 256.0), 0.0).astype(map_ref.dtype)
     chosen = jnp.where(placed, 1.0, 0.0).astype(jnp.bfloat16)
-    fetch.wait()
-    rows_ref[...] = jnp.dot(chosen, tokens[...], preferred_element_type=jnp.float32).astype(
-        rows_ref.dtype
-    )
+    fetch_tokens.wait()
+    step = rows.shape[1] // left.shape[0]
+    stores = []
+    for i in range(left.shape[0]):
+        part = pl.ds(i * step, step)
+        rows[:, part] = jnp.dot(
+            chosen, tokens[:, part], preferred_element_type=jnp.float32
+        ).astype(rows.dtype)
+        stores.append(pltpu.make_async_copy(rows.at[:, part], rows_ref.at[:, part], left.at[i]))
+        stores[-1].start()
+    for store in stores:
+        store.wait()
 
 
 def build_tables(ids, gates, tokens, experts, capacity):
@@ -57,13 +84,17 @@
             jax.ShapeDtypeStruct((experts * capacity, width), jnp.bfloat16),
             jax.ShapeDtypeStruct((experts * capacity, tok_dev), jnp.bfloat16),
         ),
-        in_specs=[whole, whole, pl.BlockSpec(memory_space=pl.ANY)],
-        out_specs=(whole, whole),
+        in_specs=[pl.BlockSpec(memory_space=pltpu.HBM)] * 3,
+        out_specs=(pl.BlockSpec(memory_space=pltpu.HBM), whole),
         scratch_shapes=[
+            pltpu.VMEM(ids.T.shape, jnp.int32),
+            pltpu.VMEM(gates.T.shape, jnp.int32),
             pltpu.VMEM((tok_dev, width), jnp.bfloat16),
-            pltpu.SemaphoreType.DMA,
+            pltpu.VMEM((experts * capacity, width), jnp.bfloat16),
+            pltpu.SemaphoreType.DMA((3,)),
+            pltpu.SemaphoreType.DMA((4,)),
         ],
-        compiler_params=pltpu.CompilerParams(vmem_limit_bytes=24 * MIB),
+        compiler_params=pltpu.CompilerParams(vmem_limit_bytes=56 * MIB),
         name="tables",
     )(ids.T, gates.T, tokens)
 
@@ -73,29 +104,32 @@
     fetch_down = pltpu.make_async_copy(down_ref, down, arrived.at[1])
     fetch_up.start()
     fetch_down.start()
-    rows = rows_ref[...]
-    for at in range(0, gate_ref.shape[1], step):
-        part = pl.ds(at, step)
-        gate_act = jnp.dot(rows, gate_ref[:, part], preferred_element_type=jnp.float32)
-        gated[:, part] = gate_act / (1.0 + jnp.exp(-gate_act))
+
+    def tiles(columns):
+        for at in range(0, columns, step):
+            for top in range(0, rows_ref.shape[0], step):
+                yield pl.ds(top, step), pl.ds(at, step)
+
+    def product(left, right):
+        return jnp.dot(left, right, preferred_element_type=jnp.float32)
+
+    for part, cols in tiles(gate_ref.shape[1]):
+        gate_act = product(rows_ref[part, :], gate_ref[:, cols])
+        gated[part, cols] = gate_act / (1.0 + jnp.exp(-gate_act))
     fetch_up.wait()
-    for at in range(0, gate_ref.shape[1], step):
-        part = pl.ds(at, step)
-        up_act = jnp.dot(rows, up[:, part], preferred_element_type=jnp.float32)
-        hidden[:, part] = (gated[:, part] * up_act).astype(hidden.dtype)
+    for part, cols in tiles(gate_ref.shape[1]):
+        up_act = product(rows_ref[part, :], up[:, cols])
+        hidden[part, cols] = (gated[part, cols] * up_act).astype(hidden.dtype)
     fetch_down.wait()
-    for at in range(0, down.shape[1], step):
-        part = pl.ds(at, step)
-        out_ref[:, part] = jnp.dot(
-            hidden[...], down[:, part], preferred_element_type=jnp.float32
-        ).astype(out_ref.dtype)
+    for part, cols in tiles(out_ref.shape[1]):
+        out_ref[part, cols] = product(hidden[part, :], down[:, cols]).astype(out_ref.dtype)
 
 
 def expert_ffn(rows, gate_mat, up_mat, down_mat):
     count, width = rows.shape
     ff = gate_mat.shape[1]
     whole = pl.BlockSpec(memory_space=pltpu.VMEM)
-    away = pl.BlockSpec(memory_space=pl.ANY)
+    away = pl.BlockSpec(memory_space=pltpu.HBM)
     return pl.pallas_call(
         lambda *refs: ffn_kernel(256, *refs),
         out_shape=jax.ShapeDtypeStruct((count, width), jnp.bfloat16),
@@ -108,7 +142,7 @@
             pltpu.VMEM((count, ff), jnp.bfloat16),
             pltpu.SemaphoreType.DMA((2,)),
         ],
-        compiler_params=pltpu.CompilerParams(vmem_limit_bytes=32 * MIB),
+        compiler_params=pltpu.CompilerParams(vmem_limit_bytes=44 * MIB),
         cost_estimate=pl.CostEstimate(
             flops=6 * count * width * ff,
             bytes_accessed=6 * width * ff + 4 * count * width,
@@ -127,18 +161,13 @@
     ).astype(out_ref.dtype)
 
 
-def combine(combine_map, results, step=512):
-    slots, width = results.shape
-    tok_dev = combine_map.shape[1]
+def combine(combine_map, results):
+    whole = pl.BlockSpec(memory_space=pltpu.VMEM)
     return pl.pallas_call(
         combine_kernel,
-        out_shape=jax.ShapeDtypeStruct((tok_dev, width), jnp.bfloat16),
-        grid=(width // step,),
-        in_specs=[
-            pl.BlockSpec((slots, tok_dev), lambda i: (0, 0)),
-            pl.BlockSpec((slots, step), lambda i: (0, i)),
-        ],
-        out_specs=pl.BlockSpec((tok_dev, step), lambda i: (0, i)),
+        out_shape=jax.ShapeDtypeStruct((combine_map.shape[1], results.shape[1]), jnp.bfloat16),
+        in_specs=[whole] * 2,
+        out_specs=whole,
         compiler_params=pltpu.CompilerParams(vmem_limit_bytes=16 * MIB),
         name="combine",
     )(combine_map, results)

time: 132 us -> 126 us (0.955)
  the two profiles are of different devices: /device:TPU:706 before, /device:TPU:514 now
where the time goes in v3:
time: 126 us
  blocking collectives  116 us (92%)
  Pallas kernels  10.1 us (8%)
    all_to_all x2, blocking collectives, exchange(): lax.all_to_all(blocks, ('node', 'chip'), split_axis=0, concat_axis=0, til...  116 us
    pallas_call x1, Pallas kernels, expert_ffn(): pl.pallas_call(lambda *refs: ffn_kernel(256, *refs), out_shape=jax.ShapeD...  5.54 us
    pallas_call x1, Pallas kernels, build_tables(): pl.pallas_call(lambda *refs: tables_kernel(experts, *refs), out_shape=(ja...  3.35 us

profile of v3, /device:TPU:514, one launch (start us, length us, event | category | flops | bytes accessed | tf_op | source)
XLA Modules:
  0.0 126.2 jit_solution(8725270123507906648)
XLA Ops:
  0.0 3.3 %tables.1 = (bf16[512,2048]{1,0:T(8,128)(2,1)}, bf16[512,64]{1,0:T(8,128)(2,1)}) custom-call(s32[8,64]{1,0:T(8,128)} %bitcast.14, s32[8,64]{1,0:T(8,128)} %bitcast.15, bf16[64,2048]{1,0:T(8,128)(2,1)} %refs_2_.1), custom_call_target="tpu_custom_call" | custom-call | tf_op jit(solution)/shard_map/tables/pallas_call | solution.py:81
  3.4 0.0 copy-start.1
  3.4 61.1 %all_to_all.10 = bf16[32,16,2048]{2,1,0:T(8,128)(2,1)S(1)} all-to-all(bf16[32,16,2048]{2,1,0:T(8,128)(2,1)} %bitcast.13), channel_id=1, replica_groups=mesh['dp'=24,'node'=8,'chip'=4] {'node','chip'}, dimensions={0} | all-to-all | bytes 4194304 | tf_op jit(solution)/shard_map/all_to_all | solution.py:185
  64.4 0.0 copy-done.1
  64.4 5.5 %ffn.1 = bf16[512,2048]{1,0:T(8,128)(2,1)S(1)} custom-call(bf16[512,2048]{1,0:T(8,128)(2,1)S(1)} %bitcast.10, bf16[2048,768]{1,0:T(8,128)(2,1)S(1)} %bitcast.12, bf16[2048,768]{1,0:T(8,128)(2,1)} %bitcast.16, bf16[768,2048]{1,0:T(8,128)(2,1)} %bitcast.17), custom_call_target="tpu_custom_call" | custom-call | flops 4831838208 | bytes 13631488 | tf_op jit(solution)/shard_map/ffn/pallas_call | solution.py:133
  70.0 0.0 copy-start
  70.0 55.0 %all_to_all.11 = bf16[32,16,2048]{2,1,0:T(8,128)(2,1)S(1)} all-to-all(bf16[32,16,2048]{2,1,0:T(8,128)(2,1)S(1)} %bitcast.11), channel_id=1, replica_groups=mesh['dp'=24,'node'=8,'chip'=4] {'node','chip'}, dimensions={0} | all-to-all | bytes 4194304 | tf_op jit(solution)/shard_map/all_to_all | solution.py:185
  125.0 0.0 copy-done
  125.0 1.2 combine.1
Async XLA Ops:
  3.4 61.1 %copy-start.1 = (bf16[1,2048,768]{2,1,0:T(8,128)(2,1)S(1)}, bf16[1,2048,768]{2,1,0:T(8,128)(2,1)}, u32[]{:S(2)}) copy-start(bf16[1,2048,768]{2,1,0:T(8,128)(2,1)} %param.9) | copy-start | bytes 9437188
  70.0 55.0 %copy-start = (bf16[512,64]{1,0:T(8,128)(2,1)S(1)}, bf16[512,64]{1,0:T(8,128)(2,1)}, u32[]{:S(2)}) copy-start(bf16[512,64]{1,0:T(8,128)(2,1)} %get-tuple-element.7.map_ref) | copy-start | bytes 196612

commit v4 on v3

v4 whole, which is shorter than its diff:
```python
import jax
import jax.numpy as jnp
from jax import lax
from jax.experimental import pallas as pl
from jax.experimental.pallas import tpu as pltpu
from jax.sharding import PartitionSpec as P

MIB = 1024 * 1024
TILE = 256
PIECES = (((2048,), (2048,)), ((256, 256, 1536), (2048,)))


def tables_kernel(experts, pieces, ids_ref, gates_ref, tokens_ref, *refs):
    rows_refs, map_ref = refs[: len(pieces)], refs[len(pieces)]
    ids_here, gates_here, tokens, rows, combine_map, arrived, left = refs[len(pieces) + 1 :]
    fetch_ids = pltpu.make_async_copy(ids_ref, ids_here, arrived.at[0])
    fetch_gates = pltpu.make_async_copy(gates_ref, gates_here, arrived.at[1])
    fetch_tokens = pltpu.make_async_copy(tokens_ref, tokens, arrived.at[2])
    fetch_ids.start()
    fetch_gates.start()
    fetch_tokens.start()
    top_count, tok_dev = ids_ref.shape
    slots = rows.shape[0]
    capacity = slots // experts
    row = lax.broadcasted_iota(jnp.int32, (slots, experts), 0)
    spread = jnp.where(
        row // capacity == lax.broadcasted_iota(jnp.int32, (slots, experts), 1), 1.0, 0.0
    ).astype(jnp.bfloat16)
    slot = lax.broadcasted_iota(jnp.int32, (slots, tok_dev), 0) % capacity
    earlier = lax.broadcasted_iota(jnp.int32, (tok_dev, tok_dev), 0) < lax.broadcasted_iota(
        jnp.int32, (tok_dev, tok_dev), 1
    )
    expert = lax.broadcasted_iota(jnp.int32, (experts, tok_dev), 0)
    fetch_ids.wait()
    ids = ids_here[...]
    named = jnp.zeros((experts, tok_dev), jnp.float32)
    for k in range(top_count):
        named = jnp.where(ids[k : k + 1, :] == expert, 1.0, named)
    rank = jnp.dot(
        named.astype(jnp.bfloat16),
        jnp.where(earlier, 1.0, 0.0).astype(jnp.bfloat16),
        preferred_element_type=jnp.float32,
    )
    rank = jnp.where(named > 0.0, rank, -1.0).astype(jnp.bfloat16)
    placed = jnp.dot(spread, rank, preferred_element_type=jnp.float32) == slot.astype(
        jnp.float32
    )
    chosen = jnp.where(placed, 1.0, 0.0).astype(jnp.bfloat16)
    fetch_tokens.wait()
    stores = []
    first = 0
    for width, rows_ref in zip(pieces, rows_refs):
        for at in range(0, width, TILE):
            part = pl.ds(first + at, TILE)
            rows[:, part] = jnp.dot(
                chosen, tokens[:, part], preferred_element_type=jnp.float32
            ).astype(rows.dtype)
            stores.append(
                pltpu.make_async_copy(
                    rows.at[:, part], rows_ref.at[:, pl.ds(at, TILE)], left.at[len(stores)]
                )
            )
            stores[-1].start()
        first += width
    fetch_gates.wait()
    gates = gates_here[...].astype(jnp.float32)
    weight = jnp.zeros((experts, tok_dev), jnp.float32)
    for k in range(top_count):
        weight = jnp.where(ids[k : k + 1, :] == expert, gates[k : k + 1, :], weight)
    share = jnp.dot(spread, weight.astype(jnp.bfloat16), preferred_element_type=jnp.float32)
    combine_map[...] = jnp.where(placed, share * (1.0 / 256.0), 0.0).astype(combine_map.dtype)
    stores.append(pltpu.make_async_copy(combine_map, map_ref, left.at[len(stores)]))
    stores[-1].start()
    for store in stores:
        store.wait()


def build_tables(ids, gates, tokens, experts, capacity, pieces):
    tok_dev, width = tokens.shape
    slots = experts * capacity
    away = pl.BlockSpec(memory_space=pltpu.HBM)
    outs = pl.pallas_call(
        lambda *refs: tables_kernel(experts, pieces, *refs),
        out_shape=[jax.ShapeDtypeStruct((slots, piece), jnp.bfloat16) for piece in pieces]
        + [jax.ShapeDtypeStruct((slots, tok_dev), jnp.bfloat16)],
        in_specs=[away] * 3,
        out_specs=[away] * (len(pieces) + 1),
        scratch_shapes=[
            pltpu.VMEM(ids.T.shape, jnp.int32),
            pltpu.VMEM(gates.T.shape, jnp.int32),
            pltpu.VMEM((tok_dev, width), jnp.bfloat16),
            pltpu.VMEM((slots, width), jnp.bfloat16),
            pltpu.VMEM((slots, tok_dev), jnp.bfloat16),
            pltpu.SemaphoreType.DMA((3,)),
            pltpu.SemaphoreType.DMA((width // TILE + 1,)),
        ],
        compiler_params=pltpu.CompilerParams(vmem_limit_bytes=56 * MIB),
        name=f"tables_{len(pieces)}",
    )(ids.T, gates.T, tokens)
    return outs[:-1], outs[-1]


def ffn_kernel(step, count, *refs):
    rows_refs, (gate_ref, up_ref, down_ref), out_refs = refs[:count], refs[count : count + 3], refs[count + 3 : -5]
    up, down, gated, hidden, arrived = refs[-5:]
    fetch_up = pltpu.make_async_copy(up_ref, up, arrived.at[0])
    fetch_down = pltpu.make_async_copy(down_ref, down, arrived.at[1])
    fetch_up.start()
    fetch_down.start()

    def tiles(columns):
        for at in range(0, columns, step):
            for top in range(0, hidden.shape[0], step):
                yield pl.ds(top, step), pl.ds(at, step)

    def product(left, right):
        return jnp.dot(left, right, preferred_element_type=jnp.float32)

    def from_rows(part, weight_ref, cols):
        total, first = None, 0
        for rows_ref in rows_refs:
            depth = rows_ref.shape[1]
            term = product(rows_ref[part, :], weight_ref[pl.ds(first, depth), cols])
            total = term if total is None else total + term
            first += depth
        return total

    for part, cols in tiles(gate_ref.shape[1]):
        gate_act = from_rows(part, gate_ref, cols)
        gated[part, cols] = gate_act / (1.0 + jnp.exp(-gate_act))
    fetch_up.wait()
    for part, cols in tiles(gate_ref.shape[1]):
        up_act = from_rows(part, up, cols)
        hidden[part, cols] = (gated[part, cols] * up_act).astype(hidden.dtype)
    fetch_down.wait()
    first = 0
    for out_ref in out_refs:
        for part, cols in tiles(out_ref.shape[1]):
            weights = down[:, pl.ds(first + cols.start, step)]
            out_ref[part, cols] = product(hidden[part, :], weights).astype(out_ref.dtype)
        first += out_ref.shape[1]


def expert_ffn(rows, gate_mat, up_mat, down_mat, pieces):
    count = rows[0].shape[0]
    width, ff = gate_mat.shape
    whole = pl.BlockSpec(memory_space=pltpu.VMEM)
    away = pl.BlockSpec(memory_space=pltpu.HBM)
    return pl.pallas_call(
        lambda *refs: ffn_kernel(256, len(rows), *refs),
        out_shape=[jax.ShapeDtypeStruct((count, piece), jnp.bfloat16) for piece in pieces],
        in_specs=[whole] * (len(rows) + 1) + [away, away],
        out_specs=[whole] * len(pieces),
        scratch_shapes=[
            pltpu.VMEM((width, ff), jnp.bfloat16),
            pltpu.VMEM((ff, width), jnp.bfloat16),
            pltpu.VMEM((count, ff), jnp.float32),
            pltpu.VMEM((count, ff), jnp.bfloat16),
            pltpu.SemaphoreType.DMA((2,)),
        ],
        compiler_params=pltpu.CompilerParams(vmem_limit_bytes=44 * MIB),
        cost_estimate=pl.CostEstimate(
            flops=6 * count * width * ff,
            bytes_accessed=6 * width * ff + 4 * count * width,
            transcendentals=count * ff,
        ),
        name=f"ffn_{len(rows)}_{len(pieces)}",
    )(*rows, gate_mat, up_mat, down_mat)


def combine_kernel(map_ref, *refs):
    results_refs, out_ref = refs[:-1], refs[-1]
    first = 0
    for results_ref in results_refs:
        width = results_ref.shape[1]
        out_ref[:, pl.ds(first, width)] = lax.dot_general(
            map_ref[...],
            results_ref[...],
            (((0,), (0,)), ((), ())),
            preferred_element_type=jnp.float32,
        ).astype(out_ref.dtype)
        first += width


def combine(combine_map, results):
    whole = pl.BlockSpec(memory_space=pltpu.VMEM)
    width = sum(result.shape[1] for result in results)
    return pl.pallas_call(
        combine_kernel,
        out_shape=jax.ShapeDtypeStruct((combine_map.shape[1], width), jnp.bfloat16),
        in_specs=[whole] * (len(results) + 1),
        out_specs=whole,
        compiler_params=pltpu.CompilerParams(vmem_limit_bytes=16 * MIB),
        name=f"combine_{len(results)}",
    )(combine_map, *results)


def layer(out_pieces, back_pieces, tokens, expert_ids, gate_fixed, w_gate, w_up, w_down):
    tok_dev, width = tokens.shape
    top_count = expert_ids.shape[1]
    experts = lax.axis_size(("node", "chip")) * w_gate.shape[0]
    capacity = tok_dev * top_count // experts
    outbound, combine_map = build_tables(
        expert_ids, gate_fixed, tokens, experts, capacity, out_pieces
    )

    def exchange(rows):
        blocks = rows.reshape(experts, capacity, rows.shape[1])
        return lax.all_to_all(
            blocks, ("node", "chip"), split_axis=0, concat_axis=0, tiled=True
        ).reshape(rows.shape)

    arrived = [exchange(rows) for rows in outbound]
    served = expert_ffn(arrived, w_gate[0], w_up[0], w_down[0], back_pieces)
    return combine(combine_map, [exchange(rows) for rows in served])


def on_device(*args):
    return lax.cond(
        lax.axis_index("dp") % 2 == 0,
        lambda *a: layer(*PIECES[0], *a),
        lambda *a: layer(*PIECES[1], *a),
        *args,
    )


def solution(mesh):
    return jax.shard_map(
        on_device,
        mesh=mesh,
        in_specs=(
            P(("dp", "node", "chip"), None),
            P(("dp", "node", "chip"), None),
            P(("dp", "node", "chip"), None),
            P(("node", "chip"), None, None),
            P(("node", "chip"), None, None),
            P(("node", "chip"), None, None),
        ),
        out_specs=P(("dp", "node", "chip"), None),
        check_vma=False,
    )
```

time: 126 us -> 116 us (0.921)
  the two profiles are of different devices: /device:TPU:514 before, /device:TPU:1 now
where the time goes in v4:
time: 116 us; the launch traced here: 115 us
  blocking collectives  105 us (91%)
  Pallas kernels  8.89 us (8%)
    all_to_all x4, blocking collectives, exchange(): lax.all_to_all(blocks, ('node', 'chip'), split_axis=0, concat_axis=0, til...  105 us
    pallas_call x1, Pallas kernels, expert_ffn(): pl.pallas_call(lambda *refs: ffn_kernel(256, len(rows), *refs), out_shape...  5.52 us
    pallas_call x1, Pallas kernels, build_tables(): pl.pallas_call(lambda *refs: tables_kernel(experts, pieces, *refs), out_s...  2.86 us

profile of v4, /device:TPU:1, one launch (start us, length us, event | category | flops | bytes accessed | tf_op | source)
XLA Modules:
  0.0 114.9 jit_solution(13184637895139868853)
XLA Ops:
  0.0 114.2 %conditional.1 = (bf16[64,2048]{1,0:T(8,128)(2,1)S(1)}) conditional(s32[]{:T(128)} %convert_element_type.3, (s32[64,8]{0,1:T(8,128)}, s32[64,8]{0,1:T(8,128)}, bf16[64,2048]{1,0:T(8,128)(2,1)}, bf16[1,2048,768]{2,1,0:T(8,128)(2,1)}, bf16[1,2048,768]{2,1,0:T(8,128)(2,1)}, /*index=5*/bf16[1,768,2048]{2,1,0:T(8,128)(2,1)}) %tuple.11, ...), branch_computations={%region_0.1_spmd, %region_1.2_spmd} | conditional | flops 4831838208 | bytes 34865216 | solution.py:219
  0.0 2.9 %tables_3.1 = (bf16[512,256]{1,0:T(8,128)(2,1)}, bf16[512,256]{1,0:T(8,128)(2,1)}, bf16[512,1536]{1,0:T(8,128)(2,1)}, bf16[512,64]{1,0:T(8,128)(2,1)}) custom-call(s32[8,64]{1,0:T(8,128)} %bitcast.34, s32[8,64]{1,0:T(8,128)} %bitcast.36, bf16[64,2048]{1,0:T(8,128)(2,1)} %get-tuple-element.34.refs_2_), custom_call_target="tpu_custom_call" | custom-call | tf_op jit(solution)/shard_map/cond/branch_0_fun/tables_3/pallas_call | solution.py:82
  2.9 0.0 copy-start.3
  2.9 21.2 %all_to_all.24 = bf16[32,16,256]{2,1,0:T(8,128)(2,1)S(1)} all-to-all(bf16[32,16,256]{2,1,0:T(8,128)(2,1)} %bitcast.33), channel_id=1, replica_groups=mesh['dp'=24,'node'=8,'chip'=4] {'node','chip'}, dimensions={0} | all-to-all | bytes 524288 | tf_op jit(solution)/shard_map/cond/branch_0_fun/all_to_all | solution.py:209
  24.1 17.4 %all_to_all.25 = bf16[32,16,256]{2,1,0:T(8,128)(2,1)S(1)} all-to-all(bf16[32,16,256]{2,1,0:T(8,128)(2,1)} %bitcast.32), channel_id=1, replica_groups=mesh['dp'=24,'node'=8,'chip'=4] {'node','chip'}, dimensions={0} | all-to-all | bytes 524288 | tf_op jit(solution)/shard_map/cond/branch_0_fun/all_to_all | solution.py:209
  41.5 28.0 %all_to_all.26 = bf16[32,16,1536]{2,1,0:T(8,128)(2,1)S(1)} all-to-all(bf16[32,16,1536]{2,1,0:T(8,128)(2,1)} %bitcast.31), channel_id=1, replica_groups=mesh['dp'=24,'node'=8,'chip'=4] {'node','chip'}, dimensions={0} | all-to-all | bytes 3145728 | tf_op jit(solution)/shard_map/cond/branch_0_fun/all_to_all | solution.py:209
  69.5 0.0 copy-done.3
  69.5 5.5 %ffn_3_1.1 = bf16[512,2048]{1,0:T(8,128)(2,1)S(1)} custom-call(bf16[512,256]{1,0:T(8,128)(2,1)S(1)} %bitcast.28, bf16[512,256]{1,0:T(8,128)(2,1)S(1)} %bitcast.29, bf16[512,1536]{1,0:T(8,128)(2,1)S(1)} %bitcast.27, bf16[2048,768]{1,0:T(8,128)(2,1)S(1)} %bitcast.38, bf16[2048,768]{1,0:T(8,128)(2,1)} %bitcast.40, bf16[768,2048]{1,0:T(8,128)(2,1)} %bitcast.42), custom_call_target="tpu_custom_call" | custom-call | flops 4831838208 | bytes 13631488 | tf_op jit(solution)/shard_map/cond/branch_0_fun/ffn_3_1/pallas_call | solution.py:149
  75.0 0.0 copy-start
  75.0 38.5 %all_to_all.27 = bf16[32,16,2048]{2,1,0:T(8,128)(2,1)S(1)} all-to-all(bf16[32,16,2048]{2,1,0:T(8,128)(2,1)S(1)} %bitcast.24), channel_id=1, replica_groups=mesh['dp'=24,'node'=8,'chip'=4] {'node','chip'}, dimensions={0} | all-to-all | bytes 4194304 | tf_op jit(solution)/shard_map/cond/branch_0_fun/all_to_all | solution.py:209
  113.5 0.0 copy-done
  113.5 0.5 combine_1.2
  114.2 0.0 copy-start.2
  114.2 0.7 copy-done.2
Async XLA Ops:
  2.9 66.6 %copy-start.3 = (bf16[1,2048,768]{2,1,0:T(8,128)(2,1)S(1)}, bf16[1,2048,768]{2,1,0:T(8,128)(2,1)}, u32[]{:S(2)}) copy-start(bf16[1,2048,768]{2,1,0:T(8,128)(2,1)} %get-tuple-element.39) | copy-start | bytes 9437188 | tf_op jit(solution)/shard_map/cond
  75.0 38.5 %copy-start = (bf16[512,64]{1,0:T(8,128)(2,1)S(1)}, bf16[512,64]{1,0:T(8,128)(2,1)}, u32[]{:S(2)}) copy-start(bf16[512,64]{1,0:T(8,128)(2,1)} %get-tuple-element.35.map_ref) | copy-start | bytes 196612 | tf_op jit(solution)/shard_map/cond
  114.2 0.7 copy-start.2

commit v5 on v4

--- a/solution.py
+++ b/solution.py
@@ -6,8 +6,8 @@
 from jax.sharding import PartitionSpec as P
 
 MIB = 1024 * 1024
-TILE = 256
-PIECES = (((2048,), (2048,)), ((256, 256, 1536), (2048,)))
+TILE = 128
+PIECES = (((2048,), (2048,)), ((128, 128, 1792), (2048,)))
 
 
 def tables_kernel(experts, pieces, ids_ref, gates_ref, tokens_ref, *refs):

time: 116 us -> 115 us (level)
  no operation moved by 1% of the time
where the time goes in v5:
time: 115 us
  blocking collectives  104 us (90%)
  Pallas kernels  9.36 us (8%)
    all_to_all x4, blocking collectives, exchange(): lax.all_to_all(blocks, ('node', 'chip'), split_axis=0, concat_axis=0, til...  104 us
    pallas_call x1, Pallas kernels, expert_ffn(): pl.pallas_call(lambda *refs: ffn_kernel(256, len(rows), *refs), out_shape...  5.85 us
    pallas_call x1, Pallas kernels, build_tables(): pl.pallas_call(lambda *refs: tables_kernel(experts, pieces, *refs), out_s...  3.01 us

profile of v5, /device:TPU:1, one launch (start us, length us, event | category | flops | bytes accessed | tf_op | source)
XLA Modules:
  0.0 114.8 jit_solution(1667622521748505177)
XLA Ops:
  0.0 114.0 %conditional.1 = (bf16[64,2048]{1,0:T(8,128)(2,1)S(1)}) conditional(s32[]{:T(128)} %convert_element_type.3, (s32[64,8]{0,1:T(8,128)}, s32[64,8]{0,1:T(8,128)}, bf16[64,2048]{1,0:T(8,128)(2,1)}, bf16[1,2048,768]{2,1,0:T(8,128)(2,1)}, bf16[1,2048,768]{2,1,0:T(8,128)(2,1)}, /*index=5*/bf16[1,768,2048]{2,1,0:T(8,128)(2,1)}) %tuple.11, ...), branch_computations={%region_0.1_spmd, %region_1.2_spmd} | conditional | flops 4831838208 | bytes 34865216 | solution.py:219
  0.0 3.0 %tables_3.1 = (bf16[512,128]{1,0:T(8,128)(2,1)}, bf16[512,128]{1,0:T(8,128)(2,1)}, bf16[512,1792]{1,0:T(8,128)(2,1)}, bf16[512,64]{1,0:T(8,128)(2,1)}) custom-call(s32[8,64]{1,0:T(8,128)} %bitcast.34, s32[8,64]{1,0:T(8,128)} %bitcast.36, bf16[64,2048]{1,0:T(8,128)(2,1)} %get-tuple-element.34.refs_2_), custom_call_target="tpu_custom_call" | custom-call | tf_op jit(solution)/shard_map/cond/branch_0_fun/tables_3/pallas_call | solution.py:82
  3.0 0.0 copy-start.3
  3.0 20.1 %all_to_all.24 = bf16[32,16,128]{2,1,0:T(8,128)(2,1)S(1)} all-to-all(bf16[32,16,128]{2,1,0:T(8,128)(2,1)} %bitcast.33), channel_id=1, replica_groups=mesh['dp'=24,'node'=8,'chip'=4] {'node','chip'}, dimensions={0} | all-to-all | bytes 262144 | tf_op jit(solution)/shard_map/cond/branch_0_fun/all_to_all | solution.py:209
  23.2 15.0 %all_to_all.25 = bf16[32,16,128]{2,1,0:T(8,128)(2,1)S(1)} all-to-all(bf16[32,16,128]{2,1,0:T(8,128)(2,1)} %bitcast.32), channel_id=1, replica_groups=mesh['dp'=24,'node'=8,'chip'=4] {'node','chip'}, dimensions={0} | all-to-all | bytes 262144 | tf_op jit(solution)/shard_map/cond/branch_0_fun/all_to_all | solution.py:209
  38.2 31.6 %all_to_all.26 = bf16[32,16,1792]{2,1,0:T(8,128)(2,1)S(1)} all-to-all(bf16[32,16,1792]{2,1,0:T(8,128)(2,1)} %bitcast.31), channel_id=1, replica_groups=mesh['dp'=24,'node'=8,'chip'=4] {'node','chip'}, dimensions={0} | all-to-all | bytes 3670016 | tf_op jit(solution)/shard_map/cond/branch_0_fun/all_to_all | solution.py:209
  69.7 0.0 copy-done.3
  69.7 5.9 %ffn_3_1.1 = bf16[512,2048]{1,0:T(8,128)(2,1)S(1)} custom-call(bf16[512,128]{1,0:T(8,128)(2,1)S(1)} %bitcast.28, bf16[512,128]{1,0:T(8,128)(2,1)S(1)} %bitcast.29, bf16[512,1792]{1,0:T(8,128)(2,1)S(1)} %bitcast.27, bf16[2048,768]{1,0:T(8,128)(2,1)S(1)} %bitcast.38, bf16[2048,768]{1,0:T(8,128)(2,1)} %bitcast.40, bf16[768,2048]{1,0:T(8,128)(2,1)} %bitcast.42), custom_call_target="tpu_custom_call" | custom-call | flops 4831838208 | bytes 13631488 | tf_op jit(solution)/shard_map/cond/branch_0_fun/ffn_3_1/pallas_call | solution.py:149
  75.6 0.0 copy-start
  75.6 37.7 %all_to_all.27 = bf16[32,16,2048]{2,1,0:T(8,128)(2,1)S(1)} all-to-all(bf16[32,16,2048]{2,1,0:T(8,128)(2,1)S(1)} %bitcast.24), channel_id=1, replica_groups=mesh['dp'=24,'node'=8,'chip'=4] {'node','chip'}, dimensions={0} | all-to-all | bytes 4194304 | tf_op jit(solution)/shard_map/cond/branch_0_fun/all_to_all | solution.py:209
  113.3 0.0 copy-done
  113.3 0.5 combine_1.2
  114.0 0.0 copy-start.2
  114.1 0.7 copy-done.2
Async XLA Ops:
  3.0 66.7 %copy-start.3 = (bf16[1,2048,768]{2,1,0:T(8,128)(2,1)S(1)}, bf16[1,2048,768]{2,1,0:T(8,128)(2,1)}, u32[]{:S(2)}) copy-start(bf16[1,2048,768]{2,1,0:T(8,128)(2,1)} %get-tuple-element.39) | copy-start | bytes 9437188 | tf_op jit(solution)/shard_map/cond
  75.6 37.7 %copy-start = (bf16[512,64]{1,0:T(8,128)(2,1)S(1)}, bf16[512,64]{1,0:T(8,128)(2,1)}, u32[]{:S(2)}) copy-start(bf16[512,64]{1,0:T(8,128)(2,1)} %get-tuple-element.35.map_ref) | copy-start | bytes 196612 | tf_op jit(solution)/shard_map/cond
  114.0 0.7 copy-start.2

commit v6 on v5

--- a/solution.py
+++ b/solution.py
@@ -7,7 +7,7 @@
 
 MIB = 1024 * 1024
 TILE = 128
-PIECES = (((2048,), (2048,)), ((128, 128, 1792), (2048,)))
+PIECES = (((2048,), (2048,)), ((128, 256, 1664), (2048,)))
 
 
 def tables_kernel(experts, pieces, ids_ref, gates_ref, tokens_ref, *refs):

time: 115 us -> 116 us (level)
  blocking collectives: 104 us -> 106 us
where the time goes in v6:
time: 116 us
  blocking collectives  106 us (91%)
  Pallas kernels  9.39 us (8%)
    all_to_all x4, blocking collectives, exchange(): lax.all_to_all(blocks, ('node', 'chip'), split_axis=0, concat_axis=0, til...  106 us
    pallas_call x1, Pallas kernels, expert_ffn(): pl.pallas_call(lambda *refs: ffn_kernel(256, len(rows), *refs), out_shape...  5.89 us
    pallas_call x1, Pallas kernels, build_tables(): pl.pallas_call(lambda *refs: tables_kernel(experts, pieces, *refs), out_s...  3 us

profile of v6, /device:TPU:1, one launch (start us, length us, event | category | flops | bytes accessed | tf_op | source)
XLA Modules:
  0.0 115.9 jit_solution(2850441810248739183)
XLA Ops:
  0.0 115.2 %conditional.1 = (bf16[64,2048]{1,0:T(8,128)(2,1)S(1)}) conditional(s32[]{:T(128)} %convert_element_type.3, (s32[64,8]{0,1:T(8,128)}, s32[64,8]{0,1:T(8,128)}, bf16[64,2048]{1,0:T(8,128)(2,1)}, bf16[1,2048,768]{2,1,0:T(8,128)(2,1)}, bf16[1,2048,768]{2,1,0:T(8,128)(2,1)}, /*index=5*/bf16[1,768,2048]{2,1,0:T(8,128)(2,1)}) %tuple.11, ...), branch_computations={%region_0.1_spmd, %region_1.2_spmd} | conditional | flops 4831838208 | bytes 34865216 | solution.py:219
  0.0 3.0 %tables_3.1 = (bf16[512,128]{1,0:T(8,128)(2,1)}, bf16[512,256]{1,0:T(8,128)(2,1)}, bf16[512,1664]{1,0:T(8,128)(2,1)}, bf16[512,64]{1,0:T(8,128)(2,1)}) custom-call(s32[8,64]{1,0:T(8,128)} %bitcast.34, s32[8,64]{1,0:T(8,128)} %bitcast.36, bf16[64,2048]{1,0:T(8,128)(2,1)} %get-tuple-element.34.refs_2_), custom_call_target="tpu_custom_call" | custom-call | tf_op jit(solution)/shard_map/cond/branch_0_fun/tables_3/pallas_call | solution.py:82
  3.0 0.0 copy-start.3
  3.0 20.1 %all_to_all.24 = bf16[32,16,128]{2,1,0:T(8,128)(2,1)S(1)} all-to-all(bf16[32,16,128]{2,1,0:T(8,128)(2,1)} %bitcast.33), channel_id=1, replica_groups=mesh['dp'=24,'node'=8,'chip'=4] {'node','chip'}, dimensions={0} | all-to-all | bytes 262144 | tf_op jit(solution)/shard_map/cond/branch_0_fun/all_to_all | solution.py:209
  23.1 17.1 %all_to_all.25 = bf16[32,16,256]{2,1,0:T(8,128)(2,1)S(1)} all-to-all(bf16[32,16,256]{2,1,0:T(8,128)(2,1)} %bitcast.32), channel_id=1, replica_groups=mesh['dp'=24,'node'=8,'chip'=4] {'node','chip'}, dimensions={0} | all-to-all | bytes 524288 | tf_op jit(solution)/shard_map/cond/branch_0_fun/all_to_all | solution.py:209
  40.3 31.4 %all_to_all.26 = bf16[32,16,1664]{2,1,0:T(8,128)(2,1)S(1)} all-to-all(bf16[32,16,1664]{2,1,0:T(8,128)(2,1)} %bitcast.31), channel_id=1, replica_groups=mesh['dp'=24,'node'=8,'chip'=4] {'node','chip'}, dimensions={0} | all-to-all | bytes 3407872 | tf_op jit(solution)/shard_map/cond/branch_0_fun/all_to_all | solution.py:209
  71.6 0.0 copy-done.3
  71.6 5.9 %ffn_3_1.1 = bf16[512,2048]{1,0:T(8,128)(2,1)S(1)} custom-call(bf16[512,128]{1,0:T(8,128)(2,1)S(1)} %bitcast.29, bf16[512,256]{1,0:T(8,128)(2,1)S(1)} %bitcast.28, bf16[512,1664]{1,0:T(8,128)(2,1)S(1)} %bitcast.27, bf16[2048,768]{1,0:T(8,128)(2,1)S(1)} %bitcast.38, bf16[2048,768]{1,0:T(8,128)(2,1)} %bitcast.40, bf16[768,2048]{1,0:T(8,128)(2,1)} %bitcast.42), custom_call_target="tpu_custom_call" | custom-call | flops 4831838208 | bytes 13631488 | tf_op jit(solution)/shard_map/cond/branch_0_fun/ffn_3_1/pallas_call | solution.py:149
  77.5 0.0 copy-start
  77.5 36.9 %all_to_all.27 = bf16[32,16,2048]{2,1,0:T(8,128)(2,1)S(1)} all-to-all(bf16[32,16,2048]{2,1,0:T(8,128)(2,1)S(1)} %bitcast.24), channel_id=1, replica_groups=mesh['dp'=24,'node'=8,'chip'=4] {'node','chip'}, dimensions={0} | all-to-all | bytes 4194304 | tf_op jit(solution)/shard_map/cond/branch_0_fun/all_to_all | solution.py:209
  114.5 0.0 copy-done
  114.5 0.5 combine_1.2
  115.2 0.0 copy-start.2
  115.2 0.7 copy-done.2
Async XLA Ops:
  3.0 68.6 %copy-start.3 = (bf16[1,2048,768]{2,1,0:T(8,128)(2,1)S(1)}, bf16[1,2048,768]{2,1,0:T(8,128)(2,1)}, u32[]{:S(2)}) copy-start(bf16[1,2048,768]{2,1,0:T(8,128)(2,1)} %get-tuple-element.39) | copy-start | bytes 9437188 | tf_op jit(solution)/shard_map/cond
  77.5 36.9 %copy-start = (bf16[512,64]{1,0:T(8,128)(2,1)S(1)}, bf16[512,64]{1,0:T(8,128)(2,1)}, u32[]{:S(2)}) copy-start(bf16[512,64]{1,0:T(8,128)(2,1)} %get-tuple-element.35.map_ref) | copy-start | bytes 196612 | tf_op jit(solution)/shard_map/cond
  115.2 0.7 copy-start.2

commit v7 on v6

--- a/solution.py
+++ b/solution.py
@@ -7,7 +7,7 @@
 
 MIB = 1024 * 1024
 TILE = 128
-PIECES = (((2048,), (2048,)), ((128, 256, 1664), (2048,)))
+PIECES = (((2048,), (1024, 1024)), ((128, 128, 1792), (2048,)))
 
 
 def tables_kernel(experts, pieces, ids_ref, gates_ref, tokens_ref, *refs):

time: 116 us -> 126 us (1.086)
  the two profiles are of different devices: /device:TPU:1 before, /device:TPU:579 now
where the time goes in v7:
time: 126 us; the launch traced here: 125 us
  blocking collectives  115 us (91%)
  Pallas kernels  9.37 us (7%)
    all_to_all x4, blocking collectives, exchange(): lax.all_to_all(blocks, ('node', 'chip'), split_axis=0, concat_axis=0, til...  115 us
    pallas_call x1, Pallas kernels, expert_ffn(): pl.pallas_call(lambda *refs: ffn_kernel(256, len(rows), *refs), out_shape...  5.85 us
    pallas_call x1, Pallas kernels, build_tables(): pl.pallas_call(lambda *refs: tables_kernel(experts, pieces, *refs), out_s...  3.01 us

profile of v7, /device:TPU:579, one launch (start us, length us, event | category | flops | bytes accessed | tf_op | source)
XLA Modules:
  0.0 125.4 jit_solution(15675712020180324417)
XLA Ops:
  0.0 124.7 %conditional.1 = (bf16[64,2048]{1,0:T(8,128)(2,1)S(1)}) conditional(s32[]{:T(128)} %convert_element_type.3, (s32[64,8]{0,1:T(8,128)}, s32[64,8]{0,1:T(8,128)}, bf16[64,2048]{1,0:T(8,128)(2,1)}, bf16[1,2048,768]{2,1,0:T(8,128)(2,1)}, bf16[1,2048,768]{2,1,0:T(8,128)(2,1)}, /*index=5*/bf16[1,768,2048]{2,1,0:T(8,128)(2,1)}) %tuple.11, ...), branch_computations={%region_0.1_spmd, %region_1.2_spmd} | conditional | flops 4831838208 | bytes 34865216 | solution.py:219
  0.0 3.0 %tables_3.1 = (bf16[512,128]{1,0:T(8,128)(2,1)}, bf16[512,128]{1,0:T(8,128)(2,1)}, bf16[512,1792]{1,0:T(8,128)(2,1)}, bf16[512,64]{1,0:T(8,128)(2,1)}) custom-call(s32[8,64]{1,0:T(8,128)} %bitcast.38, s32[8,64]{1,0:T(8,128)} %bitcast.40, bf16[64,2048]{1,0:T(8,128)(2,1)} %get-tuple-element.34.refs_2_), custom_call_target="tpu_custom_call" | custom-call | tf_op jit(solution)/shard_map/cond/branch_0_fun/tables_3/pallas_call | solution.py:82
  3.0 0.0 copy-start.3
  3.0 18.2 %all_to_all.28 = bf16[32,16,128]{2,1,0:T(8,128)(2,1)S(1)} all-to-all(bf16[32,16,128]{2,1,0:T(8,128)(2,1)} %bitcast.37), channel_id=1, replica_groups=mesh['dp'=24,'node'=8,'chip'=4] {'node','chip'}, dimensions={0} | all-to-all | bytes 262144 | tf_op jit(solution)/shard_map/cond/branch_0_fun/all_to_all | solution.py:209
  21.3 14.4 %all_to_all.29 = bf16[32,16,128]{2,1,0:T(8,128)(2,1)S(1)} all-to-all(bf16[32,16,128]{2,1,0:T(8,128)(2,1)} %bitcast.36), channel_id=1, replica_groups=mesh['dp'=24,'node'=8,'chip'=4] {'node','chip'}, dimensions={0} | all-to-all | bytes 262144 | tf_op jit(solution)/shard_map/cond/branch_0_fun/all_to_all | solution.py:209
  35.7 36.2 %all_to_all.30 = bf16[32,16,1792]{2,1,0:T(8,128)(2,1)S(1)} all-to-all(bf16[32,16,1792]{2,1,0:T(8,128)(2,1)} %bitcast.35), channel_id=1, replica_groups=mesh['dp'=24,'node'=8,'chip'=4] {'node','chip'}, dimensions={0} | all-to-all | bytes 3670016 | tf_op jit(solution)/shard_map/cond/branch_0_fun/all_to_all | solution.py:209
  71.9 0.0 copy-done.3
  71.9 5.9 %ffn_3_1.1 = bf16[512,2048]{1,0:T(8,128)(2,1)S(1)} custom-call(bf16[512,128]{1,0:T(8,128)(2,1)S(1)} %bitcast.32, bf16[512,128]{1,0:T(8,128)(2,1)S(1)} %bitcast.33, bf16[512,1792]{1,0:T(8,128)(2,1)S(1)} %bitcast.29, bf16[2048,768]{1,0:T(8,128)(2,1)S(1)} %bitcast.42, bf16[2048,768]{1,0:T(8,128)(2,1)} %bitcast.44, bf16[768,2048]{1,0:T(8,128)(2,1)} %bitcast.46), custom_call_target="tpu_custom_call" | custom-call | flops 4831838208 | bytes 13631488 | tf_op jit(solution)/shard_map/cond/branch_0_fun/ffn_3_1/pallas_call | solution.py:149
  77.8 0.0 copy-start
  77.8 46.1 %all_to_all.31 = bf16[32,16,2048]{2,1,0:T(8,128)(2,1)S(1)} all-to-all(bf16[32,16,2048]{2,1,0:T(8,128)(2,1)S(1)} %bitcast.27), channel_id=1, replica_groups=mesh['dp'=24,'node'=8,'chip'=4] {'node','chip'}, dimensions={0} | all-to-all | bytes 4194304 | tf_op jit(solution)/shard_map/cond/branch_0_fun/all_to_all | solution.py:209
  123.9 0.0 copy-done
  123.9 0.5 combine_1.1
  124.7 0.0 copy-start.2
  124.7 0.7 copy-done.2
Async XLA Ops:
  3.0 68.9 %copy-start.3 = (bf16[1,2048,768]{2,1,0:T(8,128)(2,1)S(1)}, bf16[1,2048,768]{2,1,0:T(8,128)(2,1)}, u32[]{:S(2)}) copy-start(bf16[1,2048,768]{2,1,0:T(8,128)(2,1)} %get-tuple-element.39) | copy-start | bytes 9437188 | tf_op jit(solution)/shard_map/cond
  77.8 46.1 %copy-start = (bf16[512,64]{1,0:T(8,128)(2,1)S(1)}, bf16[512,64]{1,0:T(8,128)(2,1)}, u32[]{:S(2)}) copy-start(bf16[512,64]{1,0:T(8,128)(2,1)} %get-tuple-element.35.map_ref) | copy-start | bytes 196612 | tf_op jit(solution)/shard_map/cond
  124.7 0.7 copy-start.2
